TPU v7x, 32 devices: a whole 2x2x4 slice. The times are simulated.
32 devices in a mesh: ocx: 4 (over x, core), ocy: 8 (over z, y).
Axes of the slice: x: 2, y: 2, z: 4, core: 2. Of those that a mesh axis runs over, the one named last changes fastest.
Arguments:
- ocean_state: float32 [4, 16, 32, 1024], P(None, None, 'ocx', 'ocy'), may hold values from -6 to 6
- floe_state: float32 [4, 16384], P(None, ('ocx', 'ocy')), may hold values from -6 to 6
- floe_props: float32 [2, 16384], P(None, ('ocx', 'ocy')), may hold values from 0.6 to 1.6
- contact_pairs: int32 [2, 128, 512], P(None, ('ocx', 'ocy')), may hold values from 0 to 127, as said below
- bond_ends: int32 [2, 128, 256], P(None, ('ocx', 'ocy')), may hold values from 0 to 127
- bond_broken: int32 [128, 256], P(('ocx', 'ocy')), may hold values 0 or 1
- couple_floe: int32 [32, 9, 128], P(('ocx', 'ocy')), may hold values from 0 to 511, as said below
- couple_weight: float32 [32, 9, 128], P(('ocx', 'ocy')), may hold values from 0 to 1, as said below
- couple_cell: int32 [32, 9, 128], P(('ocx', 'ocy')), may hold values from 0 to 1023, as said below
Outputs:
- ocean_next: float32 [4, 16, 32, 1024], P(None, None, 'ocx', 'ocy')
- floe_next: float32 [4, 16384], P(None, ('ocx', 'ocy'))
Inputs may be any that keep to these rules, and one draw needn't show every extreme that they name: `contact_pairs`: unused slots name one floe twice; live slots name two different floes; a tile has at most 512 live slots and some tiles of every draw have 512. `couple_floe`: every slot, used or not, names a floe of its source device. `couple_weight`: zero exactly on unused slots and positive on used ones; in each bucket the used slots come first; buckets toward blocks outside the ocean are empty; every source device has one bucket with all 128 slots used. `couple_cell`: every slot, used or not, names a surface cell of the ocean block.
All inputs are finite; a program needn't handle non-finite values. No bound on the sum of `bond_broken` on one device may be relied on, other than what follows from the above.
Results may differ from a plain program's by a relative error of at most 0.000065.
Values sent between devices are 32-bit elements; how exact they have to be, the bound alone decides.
A program may use at most 64 MiB of HBM per device.

v0:
```python
import jax
import jax.numpy as jnp
from jax import lax
from jax.sharding import PartitionSpec as P

TILE = 128
SUBSTEPS = 4


TIME_STEP = 0.05
CONTACT_STIFF = 2.0
CONTACT_DAMP = 0.2
BOND_DAMP = 0.3
DRAG_COEF = 0.5
HEAT_COEF = 0.3
SALT_COEF = 0.2
FREEZE = -1.8
DIFFUSE_SIDE = 0.15
DIFFUSE_DEPTH = 0.2
CORIOLIS = 0.3
PRESSURE_COEF = 0.1
THERMAL_EXP = 0.2
HALINE_CONTR = 0.8
EXACT = lax.Precision.HIGHEST


def with_halo(array, sides, width):
    for axis, dim in sides:
        size, length = (lax.axis_size(axis), array.shape[dim])
        up = [(i, (i + 1) % size) for i in range(size - 1)]
        down = [(j, i) for i, j in up]
        last = lax.slice_in_dim(array, length - width, length, axis=dim)
        leading = lax.slice_in_dim(array, 0, width, axis=dim)
        before = lax.ppermute(last, axis, up)
        after = lax.ppermute(leading, axis, down)
        array = jnp.concatenate([before, array, after], axis=dim)
    return array


def ocean_update(padded, forcing):
    interior = padded[:, :, 1:-1, 1:-1]
    laplace_side = (
        padded[:, :, 2:, 1:-1]
        + padded[:, :, :-2, 1:-1]
        + padded[:, :, 1:-1, 2:]
        + padded[:, :, 1:-1, :-2]
        - 4.0 * interior
    )
    above_cells = jnp.concatenate([interior[:, :1], interior[:, :-1]], axis=1)
    below_cells = jnp.concatenate([interior[:, 1:], interior[:, -1:]], axis=1)
    laplace_depth = above_cells + below_cells - 2.0 * interior
    density = HALINE_CONTR * padded[3] - THERMAL_EXP * padded[2]
    pressure = jnp.cumsum(density, axis=0)
    grad_x = 0.5 * (pressure[:, 2:, 1:-1] - pressure[:, :-2, 1:-1])
    grad_y = 0.5 * (pressure[:, 1:-1, 2:] - pressure[:, 1:-1, :-2])
    east_vel = interior[0]
    north_vel = interior[1]
    tendency = DIFFUSE_SIDE * laplace_side + DIFFUSE_DEPTH * laplace_depth
    momentum = jnp.stack(
        [
            CORIOLIS * north_vel - PRESSURE_COEF * grad_x,
            -CORIOLIS * east_vel - PRESSURE_COEF * grad_y,
        ]
    )
    tendency = tendency.at[:2].add(momentum)
    tendency = tendency.at[:, 0].add(forcing)
    return interior + tendency


def tile_table(index_list):
    floe_ids = jnp.arange(TILE, dtype=jnp.int32)
    return (index_list[:, :, None] == floe_ids[None, None, :]).astype(jnp.float32)


def pick_rows(table, field):
    return jnp.einsum(
        "tpf,ctf->ctp", table, field, precision=EXACT, preferred_element_type=jnp.float32
    )


def spread_rows(table, values):
    return jnp.einsum(
        "tpf,ctp->ctf", table, values, precision=EXACT, preferred_element_type=jnp.float32
    )


def floe_steps(
    floe_state, floe_props, contact_pairs, bond_ends, bond_broken, intersection_area, drag_sum
):
    floe_count = floe_state.shape[1]
    tile_count = floe_count // TILE
    radius = floe_props[0].reshape(1, tile_count, TILE)
    inv_mass = (1.0 / (floe_props[1] * floe_props[0] * floe_props[0])).reshape(1, tile_count, TILE)
    first_table = tile_table(contact_pairs[0])
    second_table = tile_table(contact_pairs[1])
    pair_diff = second_table - first_table
    bond_diff = tile_table(bond_ends[1]) - tile_table(bond_ends[0])
    bond_alive = (1 - bond_broken).astype(jnp.float32)[None]
    reach_sq = ((pick_rows(first_table, radius) + pick_rows(second_table, radius)) ** 2)[0]
    positions = floe_state[:2].reshape(2, tile_count, TILE)
    velocity = floe_state[2:].reshape(2, tile_count, TILE)
    drag_tiles = drag_sum.reshape(2, tile_count, TILE)
    area_tiles = intersection_area.reshape(1, tile_count, TILE)
    mean_vel = jnp.zeros_like(velocity)
    for substep in range(SUBSTEPS):
        separation = pick_rows(pair_diff, positions)
        contact_depth = jnp.maximum(1.0 - (separation[0] ** 2 + separation[1] ** 2) / reach_sq, 0.0)
        relative = pick_rows(pair_diff, velocity)
        pair_force = contact_depth * (CONTACT_DAMP * relative - CONTACT_STIFF * separation)
        bond_force = BOND_DAMP * bond_alive * pick_rows(bond_diff, velocity)
        total_force = DRAG_COEF * (drag_tiles - area_tiles * velocity)
        total_force = (
            total_force - spread_rows(pair_diff, pair_force) - spread_rows(bond_diff, bond_force)
        )
        velocity = velocity + TIME_STEP * inv_mass * total_force
        positions = positions + TIME_STEP * velocity
        mean_vel = mean_vel + velocity / SUBSTEPS
    stacked = jnp.concatenate([positions, velocity], axis=0).reshape(4, floe_count)
    return (stacked, mean_vel.reshape(2, floe_count))


def floe_side(
    floe_state, floe_props, contact_pairs, bond_ends, bond_broken, floe_index, weight, samples
):
    floe_count = floe_state.shape[1]
    intersection_area = jnp.zeros((floe_count,), jnp.float32).at[floe_index].add(weight)
    drag_sum = jnp.zeros((2, floe_count), jnp.float32).at[:, floe_index].add(weight * samples[:2])
    floe_next, mean_vel = floe_steps(
        floe_state, floe_props, contact_pairs, bond_ends, bond_broken, intersection_area, drag_sum
    )
    ice_vel = mean_vel[:, floe_index]
    stress = DRAG_COEF * weight * (ice_vel - samples[:2])
    heat_flux = HEAT_COEF * weight * (FREEZE - samples[2])
    salt_flux = SALT_COEF * weight * floe_props[1][floe_index]
    return (floe_next, jnp.concatenate([stress, heat_flux[None], salt_flux[None]], axis=0))


def cell_table(cells, cell_count):
    cell_ids = jnp.arange(cell_count, dtype=jnp.int32)
    return (cells[:, None] == cell_ids[None, :]).astype(jnp.float32)


def shards(
    ocean_state,
    floe_state,
    floe_props,
    contact_pairs,
    bond_ends,
    bond_broken,
    couple_floe,
    couple_weight,
    couple_cell,
):
    levels, width_x, width_y = (ocean_state.shape[1], ocean_state.shape[2], ocean_state.shape[3])
    cell_count = width_x * width_y
    slot_count = couple_cell.shape[2]
    surface = ocean_state[:, 0].reshape(4, cell_count)
    sampled_parts = []
    for bucket in range(9):
        table = cell_table(couple_cell[0, bucket], cell_count)
        sampled_parts.append(
            jnp.dot(surface, table.T, precision=EXACT, preferred_element_type=jnp.float32)
        )
    outgoing = jnp.stack(sampled_parts, axis=1).reshape(4, 3, 3, slot_count)
    widened = with_halo(outgoing, (("ocx", 1), ("ocy", 2)), 1)
    arrived = widened[:, ::2, ::2]
    arrived = arrived.reshape(4, 9 * slot_count)
    padded = with_halo(ocean_state, (("ocx", 2), ("ocy", 3)), 1)
    floe_index = couple_floe[0].reshape(-1)
    weight = couple_weight[0].reshape(-1)
    floe_next, flux = floe_side(
        floe_state, floe_props, contact_pairs, bond_ends, bond_broken, floe_index, weight, arrived
    )
    flux = flux.reshape(4, 3, 3, slot_count)
    widened_flux = with_halo(flux, (("ocx", 1), ("ocy", 2)), 1)
    received = widened_flux[:, ::2, ::2]
    received = received.reshape(4, 9, slot_count)
    forcing = jnp.zeros((4, cell_count), jnp.float32)
    for bucket in range(9):
        table = cell_table(couple_cell[0, bucket], cell_count)
        forcing = forcing + jnp.dot(
            received[:, bucket], table, precision=EXACT, preferred_element_type=jnp.float32
        )
    forcing = forcing.reshape(4, width_x, width_y)
    return (ocean_update(padded, forcing), floe_next)


def solution(mesh):
    in_specs = (
        P(None, None, "ocx", "ocy"),
        P(None, ("ocx", "ocy")),
        P(None, ("ocx", "ocy")),
        P(None, ("ocx", "ocy"), None),
        P(None, ("ocx", "ocy"), None),
        P(("ocx", "ocy"), None),
        P(("ocx", "ocy"), None, None),
        P(("ocx", "ocy"), None, None),
        P(("ocx", "ocy"), None, None),
    )
    out_specs = (P(None, None, "ocx", "ocy"), P(None, ("ocx", "ocy")))
    return jax.shard_map(shards, mesh=mesh, in_specs=in_specs, out_specs=out_specs, check_vma=False)
```

profile of v0, /device:TPU:1, one launch (start us, length us, event | category | flops | bytes accessed | tf_op | source)
XLA Modules:
  0.0 121.3 jit_solution(2792155702490161842)
XLA Ops:
  0.6 1.1 fusion.192
  1.7 2.0 %collective-permute-start = (f32[4,16,1,128]{3,2,1,0:T(1,128)S(1)}, f32[4,16,1,128]{3,2,1,0:T(1,128)S(1)}, u32[]{:S(2)}, u32[]{:S(2)}) collective-permute-start(f32[4,16,1,128]{3,2,1,0:T(1,128)S(1)} %get-tuple-element.38), channel_id=1, source_target_pairs={{8,0},{16,8},{24,16},{9,1},{17,9},{25,17},{10,2},{18,10},{26,18},{... | collective-permute-start | bytes 98312 | tf_op jit(solution)/shard_map/ppermute | solution.py:35
  3.7 4.5 %collective-permute-start.1 = (f32[4,16,1,128]{3,2,1,0:T(1,128)S(1)}, f32[4,16,1,128]{3,2,1,0:T(1,128)S(1)}, u32[]{:S(2)}, u32[]{:S(2)}) collective-permute-start(f32[4,16,1,128]{3,2,1,0:T(1,128)S(1)} %get-tuple-element.37), channel_id=1, source_target_pairs={{0,8},{8,16},{16,24},{1,9},{9,17},{17,25},{2,10},{10,18},{18,26},{... | collective-permute-start | bytes 98312 | tf_op jit(solution)/shard_map/ppermute | solution.py:34
  8.2 0.7 slice_bitcast_fusion.31
  9.3 0.4 fusion.40
  12.7 1.9 %collective-permute-start.5 = (f32[4,1,3,128]{3,0,2,1:T(4,128)S(1)}, f32[4,1,3,128]{3,0,2,1:T(4,128)S(1)}, u32[]{:S(2)}, u32[]{:S(2)}) collective-permute-start(f32[4,1,3,128]{3,0,2,1:T(4,128)S(1)} %get-tuple-element.46), channel_id=1, source_target_pairs={{8,0},{16,8},{24,16},{9,1},{17,9},{25,17},{10,2},{18,10},{26,18},{... | collective-permute-start | bytes 18440 | tf_op jit(solution)/shard_map/ppermute | solution.py:35
  14.6 3.6 %collective-permute-start.4 = (f32[4,1,3,128]{3,0,2,1:T(4,128)S(1)}, f32[4,1,3,128]{3,0,2,1:T(4,128)S(1)}, u32[]{:S(2)}, u32[]{:S(2)}) collective-permute-start(f32[4,1,3,128]{3,0,2,1:T(4,128)S(1)} %get-tuple-element.45), channel_id=1, source_target_pairs={{0,8},{8,16},{16,24},{1,9},{9,17},{17,25},{2,10},{10,18},{18,26},{... | collective-permute-start | bytes 18440 | tf_op jit(solution)/shard_map/ppermute | solution.py:34
  18.4 0.6 copy-done.7
  19.1 0.7 copy-done.6
  19.7 0.7 fusion.43
  20.5 0.7 fusion.42
  21.2 1.6 %convolution_bitcast_fusion.3 = f32[2,4,512]{2,0,1:T(2,128)S(1)} fusion(s32[4,512]{1,0:T(4,128)S(1)} %get-tuple-element.48, s32[4,512]{1,0:T(4,128)S(1)} %get-tuple-element.47, f32[4,512]{1,0:T(4,128)S(1)} %copy-done.8), kind=kOutput, calls=%fused_computation.32 | convolution fusion | flops 7602176 | bytes 36864 | tf_op jit(solution)/shard_map/tpf,ctf->ctp/dot_general | solution.py:76
  22.8 0.8 fusion.16
  23.6 0.6 convolution_bitcast_fusion.11
  24.3 1.6 %fusion.12 = f32[2,4,512]{2,0,1:T(2,128)S(1)} fusion(s32[4,512]{1,0:T(4,128)S(1)} %get-tuple-element.48, s32[4,512]{1,0:T(4,128)S(1)} %get-tuple-element.47, f32[2,4,512]{2,0,1:T(2,128)S(1)} %convolution_bitcast_fusion.3, f32[4,512]{1,0:T(4,128)S(1)} %bitcast.346, f32[4,512]{1,0:T(4,128)S(1)} %copy-done.8), kind=kOutput, calls=%fused_computation.31 | convolution fusion | flops 7618560 | bytes 61440 | tf_op jit(solution)/shard_map/tpf,ctf->ctp/dot_general | solution.py:76
  26.0 0.7 copy-done.3
  26.7 1.3 %collective-permute-start.7 = (f32[4,5,1,128]{3,0,2,1:T(4,128)S(1)}, f32[4,5,1,128]{3,0,2,1:T(4,128)S(1)}, u32[]{:S(2)}, u32[]{:S(2)}) collective-permute-start(f32[4,5,1,128]{3,0,2,1:T(4,128)S(1)} %get-tuple-element.42), channel_id=1, source_target_pairs={{1,0},{2,1},{3,2},{4,3},{5,4},{6,5},{7,6},{9,8},{10,9},{11,10},{12... | collective-permute-start | bytes 30728 | tf_op jit(solution)/shard_map/ppermute | solution.py:35
  28.0 4.0 %collective-permute-start.6 = (f32[4,5,1,128]{3,0,2,1:T(4,128)S(1)}, f32[4,5,1,128]{3,0,2,1:T(4,128)S(1)}, u32[]{:S(2)}, u32[]{:S(2)}) collective-permute-start(f32[4,5,1,128]{3,0,2,1:T(4,128)S(1)} %get-tuple-element.41), channel_id=1, source_target_pairs={{0,1},{1,2},{2,3},{3,4},{4,5},{5,6},{6,7},{8,9},{9,10},{10,11},{11... | collective-permute-start | bytes 30728 | tf_op jit(solution)/shard_map/ppermute | solution.py:34
  32.0 7.3 %gather_fusion.1 = f32[1152]{0:T(1024)S(1)} fusion(f32[512]{0:T(512)S(1)} %bitcast.327, s32[2048]{0:T(1024)S(1)} %pad_clamp_fusion), kind=kCustom, calls=%fused_computation.1 | custom fusion | bytes 13824 | tf_op jit(solution)/shard_map/gather | solution.py:134
  39.3 9.2 %scatter_custom_fusion.1 = f32[512]{0:T(512)S(1)} fusion(s32[1152]{0:T(1024)S(1)} %fusion.159, f32[1152]{0:T(1024)S(1)} %bitcast.333, f32[]{:T(128)} %constant.95.clone.1), kind=kCustom, calls=%fused_computation.307 | custom fusion | flops 1152 | bytes 2052 | tf_op jit(solution)/shard_map/scatter-add | solution.py:126
  49.1 8.4 %scatter_custom_fusion = f32[2,512]{0,1:T(8,128)S(1)} fusion(s32[1152]{0:T(1024)S(1)} %fusion.159, f32[2,1152]{0,1:T(8,128)S(1)} %bitcast_multiply_fusion, f32[]{:T(128)} %constant.95.clone.1), kind=kCustom, calls=%fused_computation.88 | custom fusion | flops 2304 | bytes 593924 | tf_op jit(solution)/shard_map/scatter-add | solution.py:127
  57.6 1.3 %bitcast_add_fusion.1 = (f32[2,4,128]{2,0,1:T(2,128)S(1)}, f32[2,4,128]{2,0,1:T(2,128)S(1)}) fusion(f32[4,512]{1,0:T(4,128)S(1)} %copy-done.8, f32[2,4,128]{2,0,1:T(2,128)S(1)} %convolution_bitcast_fusion.11, f32[2,4,512]{2,0,1:T(2,128)S(1)} %fusion.12, s32[4,512]{1,0:T(4,128)S(1)} %get-tuple-element.48, s32[4,512]{1,0:T(4,128)S(1)} %get-tuple-element.47, ...), kind=kOutput, calls=%fused_computation.274 | convolution fusion | flops 7611392 | bytes 61440 | tf_op jit(solution)/shard_map/tpf,ctp->ctf/dot_general | solution.py:82
  58.9 0.8 fusion.15
  59.7 0.6 convolution_bitcast_fusion.10
  60.3 1.6 %convolution_bitcast_fusion.2 = f32[2,4,512]{2,0,1:T(2,128)S(1)} fusion(f32[2,4,128]{2,0,1:T(2,128)S(1)} %get-tuple-element.66, s32[4,512]{1,0:T(4,128)S(1)} %get-tuple-element.48, s32[4,512]{1,0:T(4,128)S(1)} %get-tuple-element.47), kind=kOutput, calls=%fused_computation.27 | convolution fusion | flops 7602176 | bytes 36864 | tf_op jit(solution)/shard_map/tpf,ctf->ctp/dot_general | solution.py:76
  62.0 1.6 %fusion.9 = f32[2,4,512]{2,0,1:T(2,128)S(1)} fusion(f32[2,4,128]{2,0,1:T(2,128)S(1)} %get-tuple-element.67, s32[4,512]{1,0:T(4,128)S(1)} %get-tuple-element.48, s32[4,512]{1,0:T(4,128)S(1)} %get-tuple-element.47, f32[2,4,512]{2,0,1:T(2,128)S(1)} %convolution_bitcast_fusion.2, f32[4,512]{1,0:T(4,128)S(1)} %bitcast.347), kind=kOutput, calls=%fused_computation.26 | convolution fusion | flops 7618560 | bytes 61440 | tf_op jit(solution)/shard_map/tpf,ctf->ctp/dot_general | solution.py:76
  63.6 1.3 %fusion.28 = f32[2,4,128]{2,0,1:T(2,128)S(1)} fusion(f32[2,4,128]{2,0,1:T(2,128)S(1)} %get-tuple-element.67, f32[2,4,128]{2,0,1:T(2,128)S(1)} %convolution_bitcast_fusion.10, f32[2,4,512]{2,0,1:T(2,128)S(1)} %fusion.9, s32[4,512]{1,0:T(4,128)S(1)} %get-tuple-element.48, s32[4,512]{1,0:T(4,128)S(1)} %get-tuple-element.47, f32[2,4,128]{2,0,1:T(2,128)S(1)} %copy.16, ...), kind=kOutput, calls=%fused_computation.55 | convolution fusion | flops 7609344 | bytes 53248 | tf_op jit(solution)/shard_map/tpf,ctp->ctf/dot_general | solution.py:82
  64.9 0.8 fusion.14
  65.7 1.6 %convolution_bitcast_fusion.1 = f32[2,4,512]{2,0,1:T(2,128)S(1)} fusion(s32[4,512]{1,0:T(4,128)S(1)} %get-tuple-element.48, s32[4,512]{1,0:T(4,128)S(1)} %get-tuple-element.47, f32[2,4,128]{2,0,1:T(2,128)S(1)} %get-tuple-element.66, f32[2,4,128]{2,0,1:T(2,128)S(1)} %fusion.28), kind=kOutput, calls=%fused_computation.22 | convolution fusion | flops 7604224 | bytes 40960 | tf_op jit(solution)/shard_map/tpf,ctf->ctp/dot_general | solution.py:76
  67.3 0.6 convolution_bitcast_fusion.9
  67.9 1.6 %fusion.6 = f32[2,4,512]{2,0,1:T(2,128)S(1)} fusion(f32[2,4,128]{2,0,1:T(2,128)S(1)} %fusion.28, s32[4,512]{1,0:T(4,128)S(1)} %get-tuple-element.48, s32[4,512]{1,0:T(4,128)S(1)} %get-tuple-element.47, f32[2,4,512]{2,0,1:T(2,128)S(1)} %convolution_bitcast_fusion.1, f32[4,512]{1,0:T(4,128)S(1)} %bitcast.348), kind=kOutput, calls=%fused_computation.21 | convolution fusion | flops 7618560 | bytes 61440 | tf_op jit(solution)/shard_map/tpf,ctf->ctp/dot_general | solution.py:76
  69.6 1.3 %fusion.24 = f32[2,4,128]{2,0,1:T(2,128)S(1)} fusion(f32[2,4,128]{2,0,1:T(2,128)S(1)} %fusion.28, f32[2,4,128]{2,0,1:T(2,128)S(1)} %convolution_bitcast_fusion.9, f32[2,4,512]{2,0,1:T(2,128)S(1)} %fusion.6, s32[4,512]{1,0:T(4,128)S(1)} %get-tuple-element.48, s32[4,512]{1,0:T(4,128)S(1)} %get-tuple-element.47, f32[2,4,128]{2,0,1:T(2,128)S(1)} %copy.16, ...), kind=kOutput, calls=%fused_computation.50 | convolution fusion | flops 7609344 | bytes 53248 | tf_op jit(solution)/shard_map/tpf,ctp->ctf/dot_general | solution.py:82
  70.9 0.8 fusion.13
  71.6 1.6 %convolution_bitcast_fusion = f32[2,4,512]{2,0,1:T(2,128)S(1)} fusion(s32[4,512]{1,0:T(4,128)S(1)} %get-tuple-element.48, s32[4,512]{1,0:T(4,128)S(1)} %get-tuple-element.47, f32[2,4,128]{2,0,1:T(2,128)S(1)} %fusion.24, f32[2,4,128]{2,0,1:T(2,128)S(1)} %get-tuple-element.66, f32[2,4,128]{2,0,1:T(2,128)S(1)} %fusion.28), kind=kOutput, calls=%fused_computation.17 | convolution fusion | flops 7606272 | bytes 45056 | tf_op jit(solution)/shard_map/tpf,ctf->ctp/dot_general | solution.py:76
  73.3 0.6 convolution_bitcast_fusion.8
  73.9 1.6 %fusion.3 = f32[2,4,512]{2,0,1:T(2,128)S(1)} fusion(f32[2,4,128]{2,0,1:T(2,128)S(1)} %fusion.24, s32[4,512]{1,0:T(4,128)S(1)} %get-tuple-element.48, s32[4,512]{1,0:T(4,128)S(1)} %get-tuple-element.47, f32[2,4,512]{2,0,1:T(2,128)S(1)} %convolution_bitcast_fusion, f32[4,512]{1,0:T(4,128)S(1)} %bitcast.349), kind=kOutput, calls=%fused_computation.16 | convolution fusion | flops 7618560 | bytes 61440 | tf_op jit(solution)/shard_map/tpf,ctf->ctp/dot_general | solution.py:76
  75.6 1.3 %fusion.20 = f32[2,4,128]{2,0,1:T(2,128)S(1)} fusion(f32[2,4,128]{2,0,1:T(2,128)S(1)} %fusion.24, f32[2,4,128]{2,0,1:T(2,128)S(1)} %convolution_bitcast_fusion.8, f32[2,4,512]{2,0,1:T(2,128)S(1)} %fusion.3, s32[4,512]{1,0:T(4,128)S(1)} %get-tuple-element.48, s32[4,512]{1,0:T(4,128)S(1)} %get-tuple-element.47, f32[2,4,128]{2,0,1:T(2,128)S(1)} %copy.16, ...), kind=kOutput, calls=%fused_computation.45 | convolution fusion | flops 7609344 | bytes 53248 | tf_op jit(solution)/shard_map/tpf,ctp->ctf/dot_general | solution.py:82
  77.0 2.4 %gather_fusion = f32[1152,2]{1,0:T(8,128)S(1)} fusion(f32[2,512]{0,1:T(8,128)S(1)} %copy.20, s32[2048]{0:T(1024)S(1)} %pad_clamp_fusion), kind=kCustom, calls=%fused_computation | custom fusion | bytes 23040 | tf_op jit(solution)/shard_map/gather | solution.py:131
  79.8 1.9 %collective-permute-start.9 = (f32[4,1,3,128]{3,0,2,1:T(4,128)S(1)}, f32[4,1,3,128]{3,0,2,1:T(4,128)S(1)}, u32[]{:S(2)}, u32[]{:S(2)}) collective-permute-start(f32[4,1,3,128]{3,0,2,1:T(4,128)S(1)} %get-tuple-element.44), channel_id=1, source_target_pairs={{8,0},{16,8},{24,16},{9,1},{17,9},{25,17},{10,2},{18,10},{26,18},{... | collective-permute-start | bytes 18440 | tf_op jit(solution)/shard_map/ppermute | solution.py:35
  81.7 3.6 %collective-permute-start.8 = (f32[4,1,3,128]{3,0,2,1:T(4,128)S(1)}, f32[4,1,3,128]{3,0,2,1:T(4,128)S(1)}, u32[]{:S(2)}, u32[]{:S(2)}) collective-permute-start(f32[4,1,3,128]{3,0,2,1:T(4,128)S(1)} %get-tuple-element.43), channel_id=1, source_target_pairs={{0,8},{8,16},{16,24},{1,9},{9,17},{17,25},{2,10},{10,18},{18,26},{... | collective-permute-start | bytes 18440 | tf_op jit(solution)/shard_map/ppermute | solution.py:34
  85.3 0.6 maximum_bitcast_fusion
  86.1 1.3 %collective-permute-start.11 = (f32[4,5,1,128]{3,0,2,1:T(4,128)S(1)}, f32[4,5,1,128]{3,0,2,1:T(4,128)S(1)}, u32[]{:S(2)}, u32[]{:S(2)}) collective-permute-start(f32[4,5,1,128]{3,0,2,1:T(4,128)S(1)} %get-tuple-element.40), channel_id=1, source_target_pairs={{1,0},{2,1},{3,2},{4,3},{5,4},{6,5},{7,6},{9,8},{10,9},{11,10},{12... | collective-permute-start | bytes 30728 | tf_op jit(solution)/shard_map/ppermute | solution.py:35
  87.4 4.7 %collective-permute-start.10 = (f32[4,5,1,128]{3,0,2,1:T(4,128)S(1)}, f32[4,5,1,128]{3,0,2,1:T(4,128)S(1)}, u32[]{:S(2)}, u32[]{:S(2)}) collective-permute-start(f32[4,5,1,128]{3,0,2,1:T(4,128)S(1)} %get-tuple-element.39), channel_id=1, source_target_pairs={{0,1},{1,2},{2,3},{3,4},{4,5},{5,6},{6,7},{8,9},{9,10},{10,11},{11... | collective-permute-start | bytes 30728 | tf_op jit(solution)/shard_map/ppermute | solution.py:34
  92.4 4.3 %collective-permute-start.3 = (f32[4,16,10,1]{3,2,1,0:T(8,128)S(1)}, f32[4,16,10,1]{3,2,1,0:T(8,128)S(1)}, u32[]{:S(2)}, u32[]{:S(2)}) collective-permute-start(f32[4,16,10,1]{3,2,1,0:T(8,128)S(1)} %get-tuple-element.31), channel_id=1, source_target_pairs={{0,1},{1,2},{2,3},{3,4},{4,5},{5,6},{6,7},{8,9},{9,10},{10,11},{11... | collective-permute-start | bytes 7688 | tf_op jit(solution)/shard_map/ppermute | solution.py:34
  96.7 1.3 %collective-permute-start.2 = (f32[4,16,10,1]{3,2,1,0:T(8,128)S(1)}, f32[4,16,10,1]{3,2,1,0:T(8,128)S(1)}, u32[]{:S(2)}, u32[]{:S(2)}) collective-permute-start(f32[4,16,10,1]{3,2,1,0:T(8,128)S(1)} %get-tuple-element.30), channel_id=1, source_target_pairs={{1,0},{2,1},{3,2},{4,3},{5,4},{6,5},{7,6},{9,8},{10,9},{11,10},{12... | collective-permute-start | bytes 7688 | tf_op jit(solution)/shard_map/ppermute | solution.py:35
  101.2 18.4 %collective-permute-done.3 = f32[4,16,10,1]{3,2,1,0:T(8,128)S(1)} collective-permute-done((f32[4,16,10,1]{3,2,1,0:T(8,128)S(1)}, f32[4,16,10,1]{3,2,1,0:T(8,128)S(1)}, u32[]{:S(2)}, u32[]{:S(2)}) %collective-permute-start.3) | collective-permute-done | bytes 2592 | tf_op jit(solution)/shard_map/ppermute | solution.py:34
  120.1 0.5 fusion.90
  120.6 0.7 add.160
  (88 shorter events, 8.9 us)
Async XLA Ops:
  1.7 90.4 %collective-permute-start = (f32[4,16,1,128]{3,2,1,0:T(1,128)S(1)}, f32[4,16,1,128]{3,2,1,0:T(1,128)S(1)}, u32[]{:S(2)}, u32[]{:S(2)}) collective-permute-start(f32[4,16,1,128]{3,2,1,0:T(1,128)S(1)} %get-tuple-element.38), channel_id=1, source_target_pairs={{8,0},{16,8},{24,16},{9,1},{17,9},{25,17},{10,2},{18,10},{26,18},{... | collective-permute-start | bytes 98312 | tf_op jit(solution)/shard_map/ppermute | solution.py:35
  3.7 5.2 %copy-start.4 = (s32[1,9,128]{2,0,1:T(1,128)S(1)}, s32[1,9,128]{2,0,1:T(1,128)}, u32[]{:S(2)}) copy-start(s32[1,9,128]{2,0,1:T(1,128)} %param.21) | copy-start | bytes 13828
  3.7 88.4 %collective-permute-start.1 = (f32[4,16,1,128]{3,2,1,0:T(1,128)S(1)}, f32[4,16,1,128]{3,2,1,0:T(1,128)S(1)}, u32[]{:S(2)}, u32[]{:S(2)}) collective-permute-start(f32[4,16,1,128]{3,2,1,0:T(1,128)S(1)} %get-tuple-element.37), channel_id=1, source_target_pairs={{0,8},{8,16},{16,24},{1,9},{9,17},{17,25},{2,10},{10,18},{18,26},{... | collective-permute-start | bytes 98312 | tf_op jit(solution)/shard_map/ppermute | solution.py:34
  11.4 6.9 %copy-start = (f32[4,16,8,128]{3,2,1,0:T(8,128)S(1)}, f32[4,16,8,128]{3,2,1,0:T(8,128)}, u32[]{:S(2)}) copy-start(f32[4,16,8,128]{3,2,1,0:T(8,128)} %param.13) | copy-start | bytes 786436
  12.7 14.0 %collective-permute-start.5 = (f32[4,1,3,128]{3,0,2,1:T(4,128)S(1)}, f32[4,1,3,128]{3,0,2,1:T(4,128)S(1)}, u32[]{:S(2)}, u32[]{:S(2)}) collective-permute-start(f32[4,1,3,128]{3,0,2,1:T(4,128)S(1)} %get-tuple-element.46), channel_id=1, source_target_pairs={{8,0},{16,8},{24,16},{9,1},{17,9},{25,17},{10,2},{18,10},{26,18},{... | collective-permute-start | bytes 18440 | tf_op jit(solution)/shard_map/ppermute | solution.py:35
  14.6 3.7 %copy-start.5 = (f32[1,9,128]{2,0,1:T(1,128)S(1)}, f32[1,9,128]{2,0,1:T(1,128)}, u32[]{:S(2)}) copy-start(f32[1,9,128]{2,0,1:T(1,128)} %param.20) | copy-start | bytes 13828
  14.6 12.0 %collective-permute-start.4 = (f32[4,1,3,128]{3,0,2,1:T(4,128)S(1)}, f32[4,1,3,128]{3,0,2,1:T(4,128)S(1)}, u32[]{:S(2)}, u32[]{:S(2)}) collective-permute-start(f32[4,1,3,128]{3,0,2,1:T(4,128)S(1)} %get-tuple-element.45), channel_id=1, source_target_pairs={{0,8},{8,16},{16,24},{1,9},{9,17},{17,25},{2,10},{10,18},{18,26},{... | collective-permute-start | bytes 18440 | tf_op jit(solution)/shard_map/ppermute | solution.py:34
  18.3 0.7 copy-start.7
  18.3 0.7 copy-start.2
  19.0 0.7 copy-start.1
  19.1 0.7 copy-start.6
  20.5 0.7 copy-start.8
  25.9 0.7 copy-start.3
  26.7 21.8 %collective-permute-start.7 = (f32[4,5,1,128]{3,0,2,1:T(4,128)S(1)}, f32[4,5,1,128]{3,0,2,1:T(4,128)S(1)}, u32[]{:S(2)}, u32[]{:S(2)}) collective-permute-start(f32[4,5,1,128]{3,0,2,1:T(4,128)S(1)} %get-tuple-element.42), channel_id=1, source_target_pairs={{1,0},{2,1},{3,2},{4,3},{5,4},{6,5},{7,6},{9,8},{10,9},{11,10},{12... | collective-permute-start | bytes 30728 | tf_op jit(solution)/shard_map/ppermute | solution.py:35
  28.0 20.6 %collective-permute-start.6 = (f32[4,5,1,128]{3,0,2,1:T(4,128)S(1)}, f32[4,5,1,128]{3,0,2,1:T(4,128)S(1)}, u32[]{:S(2)}, u32[]{:S(2)}) collective-permute-start(f32[4,5,1,128]{3,0,2,1:T(4,128)S(1)} %get-tuple-element.41), channel_id=1, source_target_pairs={{0,1},{1,2},{2,3},{3,4},{4,5},{5,6},{6,7},{8,9},{9,10},{10,11},{11... | collective-permute-start | bytes 30728 | tf_op jit(solution)/shard_map/ppermute | solution.py:34
  79.8 6.2 %collective-permute-start.9 = (f32[4,1,3,128]{3,0,2,1:T(4,128)S(1)}, f32[4,1,3,128]{3,0,2,1:T(4,128)S(1)}, u32[]{:S(2)}, u32[]{:S(2)}) collective-permute-start(f32[4,1,3,128]{3,0,2,1:T(4,128)S(1)} %get-tuple-element.44), channel_id=1, source_target_pairs={{8,0},{16,8},{24,16},{9,1},{17,9},{25,17},{10,2},{18,10},{26,18},{... | collective-permute-start | bytes 18440 | tf_op jit(solution)/shard_map/ppermute | solution.py:35
  81.7 4.4 %collective-permute-start.8 = (f32[4,1,3,128]{3,0,2,1:T(4,128)S(1)}, f32[4,1,3,128]{3,0,2,1:T(4,128)S(1)}, u32[]{:S(2)}, u32[]{:S(2)}) collective-permute-start(f32[4,1,3,128]{3,0,2,1:T(4,128)S(1)} %get-tuple-element.43), channel_id=1, source_target_pairs={{0,8},{8,16},{16,24},{1,9},{9,17},{17,25},{2,10},{10,18},{18,26},{... | collective-permute-start | bytes 18440 | tf_op jit(solution)/shard_map/ppermute | solution.py:34
  86.1 11.9 %collective-permute-start.11 = (f32[4,5,1,128]{3,0,2,1:T(4,128)S(1)}, f32[4,5,1,128]{3,0,2,1:T(4,128)S(1)}, u32[]{:S(2)}, u32[]{:S(2)}) collective-permute-start(f32[4,5,1,128]{3,0,2,1:T(4,128)S(1)} %get-tuple-element.40), channel_id=1, source_target_pairs={{1,0},{2,1},{3,2},{4,3},{5,4},{6,5},{7,6},{9,8},{10,9},{11,10},{12... | collective-permute-start | bytes 30728 | tf_op jit(solution)/shard_map/ppermute | solution.py:35
  87.4 10.6 %collective-permute-start.10 = (f32[4,5,1,128]{3,0,2,1:T(4,128)S(1)}, f32[4,5,1,128]{3,0,2,1:T(4,128)S(1)}, u32[]{:S(2)}, u32[]{:S(2)}) collective-permute-start(f32[4,5,1,128]{3,0,2,1:T(4,128)S(1)} %get-tuple-element.39), channel_id=1, source_target_pairs={{0,1},{1,2},{2,3},{3,4},{4,5},{5,6},{6,7},{8,9},{9,10},{10,11},{11... | collective-permute-start | bytes 30728 | tf_op jit(solution)/shard_map/ppermute | solution.py:34
  92.4 27.1 %collective-permute-start.3 = (f32[4,16,10,1]{3,2,1,0:T(8,128)S(1)}, f32[4,16,10,1]{3,2,1,0:T(8,128)S(1)}, u32[]{:S(2)}, u32[]{:S(2)}) collective-permute-start(f32[4,16,10,1]{3,2,1,0:T(8,128)S(1)} %get-tuple-element.31), channel_id=1, source_target_pairs={{0,1},{1,2},{2,3},{3,4},{4,5},{5,6},{6,7},{8,9},{9,10},{10,11},{11... | collective-permute-start | bytes 7688 | tf_op jit(solution)/shard_map/ppermute | solution.py:34
  96.7 22.8 %collective-permute-start.2 = (f32[4,16,10,1]{3,2,1,0:T(8,128)S(1)}, f32[4,16,10,1]{3,2,1,0:T(8,128)S(1)}, u32[]{:S(2)}, u32[]{:S(2)}) collective-permute-start(f32[4,16,10,1]{3,2,1,0:T(8,128)S(1)} %get-tuple-element.30), channel_id=1, source_target_pairs={{1,0},{2,1},{3,2},{4,3},{5,4},{6,5},{7,6},{9,8},{10,9},{11,10},{12... | collective-permute-start | bytes 7688 | tf_op jit(solution)/shard_map/ppermute | solution.py:35
where the time goes:
time: 122 us; the launch traced here: 121 us
  starting transfers between devices  34.4 us (28%)
  matrix products  31.9 us (26%)
  other arithmetic  20.6 us (17%)
  waiting for transfers between devices  18.5 us (15%)
  local copies, waits for them, and re-layouts  14.6 us (12%)
  between operations  1.3 us (1%)
    ppermute x6, starting transfers between devices, with_halo(): before = lax.ppermute(last, axis, up)  24.7 us
    ppermute x6, waiting for transfers between devices, with_halo(): before = lax.ppermute(last, axis, up)  18.5 us
    dot_general x14, matrix products, pick_rows(): jnp.einsum('tpf,ctf->ctp', table, field, precision=EXACT, preferred_eleme...  17.4 us
    ppermute x6, starting transfers between devices, with_halo(): after = lax.ppermute(leading, axis, down)  9.69 us
    scatter-add x1, other arithmetic, floe_side(): jnp.zeros((floe_count,), jnp.float32).at[floe_index].add(weight)  9.18 us
    scatter-add x1, other arithmetic, floe_side(): jnp.zeros((2, floe_count), jnp.float32).at[:, floe_index]  8.4 us
    dot_general x8, matrix products, spread_rows(): jnp.einsum('tpf,ctp->ctf', table, values, precision=EXACT, preferred_elem...  7.63 us
    gather x2, local copies, waits for them, and re-layouts, floe_side(): salt_flux = SALT_COEF * weight * floe_props[1][floe_index]  7.3 us
  transfers between devices with their start and end apart: 12, of which 2 were waited for; matrix products, arithmetic and copies ran while one was open for 51% of the time, Pallas kernels for 0%

commit v1 on v0

v1 whole, which is shorter than its diff:
```python
import functools

import jax
import jax.numpy as jnp
from jax import lax
from jax.experimental import pallas as pl
from jax.experimental.pallas import tpu as pltpu
from jax.sharding import PartitionSpec as P

SUBSTEPS = 4
TIME_STEP = 0.05
CONTACT_STIFF = 2.0
CONTACT_DAMP = 0.2
BOND_DAMP = 0.3
DRAG_COEF = 0.5
HEAT_COEF = 0.3
SALT_COEF = 0.2
FREEZE = -1.8
DIFFUSE_SIDE = 0.15
DIFFUSE_DEPTH = 0.2
CORIOLIS = 0.3
PRESSURE_COEF = 0.1
THERMAL_EXP = 0.2
HALINE_CONTR = 0.8
MESH = pl.DeviceIdType.MESH
F32 = jnp.float32
BF16 = jnp.bfloat16
CENTRE = 4


def lane_gather(field, index):
    return lax.gather(
        field,
        index[..., None],
        lax.GatherDimensionNumbers(
            offset_dims=(),
            collapsed_slice_dims=(1,),
            start_index_map=(1,),
            operand_batching_dims=(0,),
            start_indices_batching_dims=(0,),
        ),
        slice_sizes=(1, 1),
        mode=lax.GatherScatterMode.PROMISE_IN_BOUNDS,
    )


def split(values):
    high = values.astype(BF16).astype(F32)
    return jnp.concatenate([high, values - high], axis=0).astype(BF16)


def product(values, table):
    return lax.dot_general(
        values, table, (((1,), (1,)), ((), ())), preferred_element_type=F32
    )


def hot(mask):
    return jnp.where(mask, 1.0, 0.0).astype(F32)


def kernel(
    mesh_shape,
    ocean,
    floe_state,
    floe_props,
    contact,
    bonds,
    broken,
    c_floe,
    c_weight,
    c_cell,
    ocean_out,
    floe_out,
    msg,
    msg_in,
    flux,
    flux_in,
    row_out,
    row_in,
    col_out,
    col_in,
    pair_table,
    floe_table,
    cell_table,
    state,
    props,
    tend,
    msg_send,
    msg_recv,
    flux_send,
    flux_recv,
    halo_send,
    halo_recv,
):
    size_x, size_y = mesh_shape
    fields, levels, width_x, width_y = ocean.shape
    planes = fields * levels
    buckets, slots = c_cell.shape[1], c_cell.shape[2]
    tiles, pairs = contact.shape[1], contact.shape[2]
    bond_count = bonds.shape[2]
    tile = floe_state.shape[1] // tiles
    rows = 2 * tiles
    at_x, at_y = lax.axis_index("ocx"), lax.axis_index("ocy")

    inside = []
    for n in range(buckets):
        dx, dy = n // 3 - 1, n % 3 - 1
        ok_x = {-1: at_x > 0, 0: at_x >= 0, 1: at_x < size_x - 1}[dx]
        ok_y = {-1: at_y > 0, 0: at_y >= 0, 1: at_y < size_y - 1}[dy]
        inside.append(jnp.logical_and(ok_x, ok_y))
    others = [n for n in range(buckets) if n != CENTRE]
    sides = [1, 7, 3, 5]

    def place(n):
        return (at_x + (n // 3 - 1), at_y + (n % 3 - 1))

    barrier = pltpu.get_barrier_semaphore()
    for n in others:

        @pl.when(inside[n])
        def _(n=n):
            pl.semaphore_signal(barrier, inc=1, device_id=place(n), device_id_type=MESH)

    def copy(src, dst, send, recv, n):
        return pltpu.make_async_remote_copy(
            src_ref=src,
            dst_ref=dst,
            send_sem=send,
            recv_sem=recv,
            device_id=place(n),
            device_id_type=MESH,
        )

    def msg_copy(n):
        return copy(msg.at[n], msg_in.at[8 - n], msg_send.at[n], msg_recv.at[8 - n], n)

    def flux_copy(n):
        return copy(flux.at[n], flux_in.at[8 - n], flux_send.at[n], flux_recv.at[8 - n], n)

    def halo_copy(side):
        pair = side // 2
        src, dst = (row_out, row_in) if pair == 0 else (col_out, col_in)
        mine, there = side % 2, 1 - side % 2
        return copy(
            src.at[mine],
            dst.at[there],
            halo_send.at[side],
            halo_recv.at[2 * pair + there],
            sides[side],
        )

    def msg_arrival(n):
        return copy(msg.at[8 - n], msg_in.at[n], msg_send.at[8 - n], msg_recv.at[n], n)

    def flux_arrival(n):
        return copy(flux.at[8 - n], flux_in.at[n], flux_send.at[8 - n], flux_recv.at[n], n)

    def halo_arrival(side):
        pair = side // 2
        src, dst = (row_out, row_in) if pair == 0 else (col_out, col_in)
        return copy(
            src.at[1 - side % 2],
            dst.at[side % 2],
            halo_send.at[side],
            halo_recv.at[side],
            sides[side],
        )

    row8 = lax.broadcasted_iota(jnp.int32, (8, width_y), 0)
    lane8 = lax.broadcasted_iota(jnp.int32, (8, width_y), 1)
    low = row8 < tiles
    row_tile = jnp.where(low, row8, row8 - tiles)

    def wide(ref_row):
        return jnp.broadcast_to(ref_row, (8, slots))

    for t in range(tiles):
        lanes = pl.ds(t * tile, tile)
        for c in range(2):
            state[0, pl.ds(c * tiles + t, 1), :] = floe_state[pl.ds(c, 1), lanes]
            state[1, pl.ds(c * tiles + t, 1), :] = floe_state[pl.ds(2 + c, 1), lanes]
            props[0, pl.ds(c * tiles + t, 1), :] = floe_props[pl.ds(0, 1), lanes]
            props[1, pl.ds(c * tiles + t, 1), :] = floe_props[pl.ds(1, 1), lanes]
    east, north = ocean[0, 0], ocean[1, 0]
    thick = props[1]
    floe_lane, floe_mask = [], []
    for n in range(buckets):
        cell = wide(c_cell[0, pl.ds(n, 1), :])
        cell_row, cell_lane = cell // width_y, cell % width_y
        floe = wide(c_floe[0, pl.ds(n, 1), :])
        floe_lane.append(floe % tile)
        floe_mask.append(floe // tile == row_tile)
        weight = wide(c_weight[0, pl.ds(n, 1), :])
        here = cell_row == row8
        first = jnp.where(here, lane_gather(east, cell_lane), 0.0)
        second = jnp.where(here, lane_gather(north, cell_lane), 0.0)
        first = first + pltpu.roll(first, 4, 0)
        second = second + pltpu.roll(second, 4, 0)
        both = jnp.where(low, first, second)
        both = both + pltpu.roll(both, 7, 0)
        both = both + pltpu.roll(both, 6, 0)
        msg[n] = both
        other = jnp.where(floe_mask[n], lane_gather(thick, floe_lane[n]), 0.0)
        other = other + pltpu.roll(other, 7, 0)
        other = other + pltpu.roll(other, 6, 0)
        msg[n, pl.ds(1, 1), :] = weight[0:1]
        msg[n, pl.ds(2, 1), :] = weight[0:1] * other[0:1]

    pl.semaphore_wait(barrier, sum(inside[n].astype(jnp.int32) for n in others))
    for n in others:

        @pl.when(inside[n])
        def _(n=n):
            msg_copy(n).start()

    msg_in[CENTRE] = msg[CENTRE]

    flat = ocean.reshape(planes * width_x, width_y)
    row_out[0] = flat[pl.ds(0, planes, stride=width_x), :]
    row_out[1] = flat[pl.ds(width_x - 1, planes, stride=width_x), :]
    lanes_f = lax.broadcasted_iota(jnp.int32, (fields, 8, width_y), 2)
    west = jnp.zeros((fields, 8, width_y), F32)
    side_e = jnp.zeros((fields, 8, width_y), F32)
    for k in range(levels):
        level = ocean[:, k]
        west = jnp.where(lanes_f == k, pltpu.roll(level, k, 2) if k else level, west)
        side_e = jnp.where(lanes_f == k, pltpu.roll(level, k + 1, 2), side_e)
    col_out[0] = west
    col_out[1] = side_e
    for side in range(4):

        @pl.when(inside[sides[side]])
        def _(side=side):
            halo_copy(side).start()

    low_row = lax.broadcasted_iota(jnp.int32, (tile, slots), 0)
    for n in range(buckets):
        floe = c_floe[0, pl.ds(n, 1), :] % tile
        cell = c_cell[0, pl.ds(n, 1), :] % width_y
        lanes = pl.ds(n * slots, slots)
        floe_table[:, lanes] = hot(low_row == floe).astype(BF16)
        cell_table[:, lanes] = hot(low_row == cell).astype(BF16)
    span = 128
    contact_chunks, bond_chunks = pairs // span, bond_count // span
    wide_row = lax.broadcasted_iota(jnp.int32, (tile, span), 0)
    for t in range(tiles):
        for c in range(contact_chunks + bond_chunks):
            ref, at = (contact, c) if c < contact_chunks else (bonds, c - contact_chunks)
            lanes = pl.ds(at * span, span)
            head = ref[0, pl.ds(t, 1), lanes]
            tail = ref[1, pl.ds(t, 1), lanes]
            pair_table[pl.ds(t * tile, tile), pl.ds(c * span, span)] = (
                hot(wide_row == head) - hot(wide_row == tail)
            ).astype(BF16)

    def twice(array):
        return jnp.concatenate([array, array], axis=0)

    positions, velocity = state[0], state[1]
    radius = props[0]
    inv_mass = TIME_STEP / (thick * radius * radius)
    ends, inv_reach = [], []
    for c in range(contact_chunks):
        lanes = pl.ds(c * span, span)
        head, tail = twice(contact[0, :, lanes]), twice(contact[1, :, lanes])
        reach = lane_gather(radius, head) + lane_gather(radius, tail)
        ends.append((head, tail))
        inv_reach.append(1.0 / (reach * reach))
    bond_ends, bond_coef = [], []
    for c in range(bond_chunks):
        lanes = pl.ds(c * span, span)
        bond_ends.append((twice(bonds[0, :, lanes]), twice(bonds[1, :, lanes])))
        bond_coef.append(BOND_DAMP * (1 - twice(broken[:, lanes])).astype(F32))

    def contact_force(positions, velocity):
        forces = []
        for (head, tail), inv in zip(ends, inv_reach):
            separation = lane_gather(positions, tail) - lane_gather(positions, head)
            relative = lane_gather(velocity, tail) - lane_gather(velocity, head)
            square = separation * separation
            square = square + pltpu.roll(square, tiles, 0)
            depth = jnp.maximum(1.0 - square * inv, 0.0)
            forces.append(depth * (CONTACT_DAMP * relative - CONTACT_STIFF * separation))
        for (head, tail), coef in zip(bond_ends, bond_coef):
            forces.append(coef * (lane_gather(velocity, tail) - lane_gather(velocity, head)))
        spread = product(split(jnp.concatenate(forces, axis=1)), pair_table[...])
        spread = spread[:rows] + spread[rows:]
        total = jnp.zeros((rows, tile), F32)
        for t in range(tiles):
            total = jnp.where(row_tile == t, spread[:, t * tile : (t + 1) * tile], total)
        return total

    force = contact_force(positions, velocity)

    def per_floe(values):
        total = product(split(jnp.concatenate(values, axis=1)), floe_table[...])
        return total[:rows] + total[rows:]

    weights = [wide(c_weight[0, pl.ds(n, 1), :]) for n in range(buckets)]
    masked = [jnp.where(m, w, 0.0) for m, w in zip(floe_mask, weights)]
    area = DRAG_COEF * per_floe(masked)

    for n in others:

        @pl.when(inside[n])
        def _(n=n):
            msg_arrival(n).wait_recv()

        @pl.when(jnp.logical_not(inside[n]))
        def _(n=n):
            msg_in[n] = jnp.zeros((8, slots), F32)

    samples = [
        jnp.where(low, wide(msg_in[n, pl.ds(0, 1), :]), wide(msg_in[n, pl.ds(4, 1), :]))
        for n in range(buckets)
    ]
    drag = DRAG_COEF * per_floe([m * s for m, s in zip(masked, samples)])

    mean_vel = jnp.zeros_like(velocity)
    for substep in range(SUBSTEPS):
        if substep:
            force = contact_force(positions, velocity)
        velocity = velocity + inv_mass * (drag - area * velocity + force)
        positions = positions + TIME_STEP * velocity
        mean_vel = mean_vel + velocity / SUBSTEPS

    for n in range(buckets):
        speed = jnp.where(floe_mask[n], lane_gather(mean_vel, floe_lane[n]), 0.0)
        speed = speed + pltpu.roll(speed, 7, 0)
        speed = speed + pltpu.roll(speed, 6, 0)
        flux[n] = weights[n] * speed
    for n in others:

        @pl.when(inside[n])
        def _(n=n):
            flux_copy(n).start()

    flux_in[CENTRE] = flux[CENTRE]
    state[0] = positions
    state[1] = velocity
    for t in range(tiles):
        lanes = pl.ds(t * tile, tile)
        for c in range(2):
            floe_out[pl.ds(c, 1), lanes] = state[0, pl.ds(c * tiles + t, 1), :]
            floe_out[pl.ds(2 + c, 1), lanes] = state[1, pl.ds(c * tiles + t, 1), :]

    here = [
        c_cell[0, pl.ds(n, 1), :] // width_y == row8 for n in range(buckets)
    ]

    def per_cell(ref, first, second):
        values = [
            jnp.concatenate(
                [
                    jnp.where(here[n], wide(ref[n, pl.ds(first, 1), :]), 0.0),
                    jnp.where(here[n], wide(ref[n, pl.ds(second, 1), :]), 0.0),
                ],
                axis=0,
            )
            for n in range(buckets)
        ]
        total = product(split(jnp.concatenate(values, axis=1)), cell_table[...])
        total = total[:16] + total[16:]
        return total[:8], total[8:]

    cover, salt = per_cell(msg_in, 1, 2)

    for side in range(4):

        @pl.when(inside[sides[side]])
        def _(side=side):
            halo_arrival(side).wait_recv()

        @pl.when(jnp.logical_not(inside[sides[side]]))
        def _(side=side):
            dst = row_in if side < 2 else col_in
            dst[side % 2] = jnp.zeros(dst.shape[1:], F32)

    rows_f = lax.broadcasted_iota(jnp.int32, (fields, 8, width_y), 1)
    top, bottom = rows_f == 0, rows_f == width_x - 1
    leftmost, rightmost = lanes_f == 0, lanes_f == width_y - 1
    sum_x = jnp.zeros((8, width_y), F32)
    sum_y = jnp.zeros((8, width_y), F32)
    for k in range(levels):
        level = ocean[:, k]
        before = jnp.stack([row_in[0, pl.ds(f * levels + k, 1), :] for f in range(fields)])
        after = jnp.stack([row_in[1, pl.ds(f * levels + k, 1), :] for f in range(fields)])
        up = jnp.where(top, before, pltpu.roll(level, 1, 1))
        down = jnp.where(bottom, after, pltpu.roll(level, width_x - 1, 1))
        left_in = pltpu.roll(col_in[0], width_y - k, 2) if k else col_in[0]
        right_in = pltpu.roll(col_in[1], width_y - 1 - k, 2)
        left = jnp.where(leftmost, left_in, pltpu.roll(level, 1, 2))
        right = jnp.where(rightmost, right_in, pltpu.roll(level, width_y - 1, 2))
        above = ocean[:, max(k - 1, 0)]
        below = ocean[:, min(k + 1, levels - 1)]
        centre = 1.0 - 4.0 * DIFFUSE_SIDE - 2.0 * DIFFUSE_DEPTH
        new = (
            centre * level
            + DIFFUSE_SIDE * (up + down + left + right)
            + DIFFUSE_DEPTH * (above + below)
        )
        slope_x, slope_y = down - up, right - left
        sum_x = sum_x + (HALINE_CONTR * slope_x[3] - THERMAL_EXP * slope_x[2])
        sum_y = sum_y + (HALINE_CONTR * slope_y[3] - THERMAL_EXP * slope_y[2])
        ocean_out[0, k] = new[0] + CORIOLIS * level[1] - (0.5 * PRESSURE_COEF) * sum_x
        ocean_out[1, k] = new[1] - CORIOLIS * level[0] - (0.5 * PRESSURE_COEF) * sum_y
        if k == 0:
            ocean_out[2, k] = new[2] + HEAT_COEF * (FREEZE - level[2]) * cover
            ocean_out[3, k] = new[3] + SALT_COEF * salt
        else:
            ocean_out[2, k] = new[2]
            ocean_out[3, k] = new[3]

    for n in others:

        @pl.when(inside[n])
        def _(n=n):
            flux_arrival(n).wait_recv()

        @pl.when(jnp.logical_not(inside[n]))
        def _(n=n):
            flux_in[n] = jnp.zeros((8, slots), F32)

    push_x, push_y = per_cell(flux_in, 0, 4)
    ocean_out[0, 0] += DRAG_COEF * (push_x - ocean[0, 0] * cover)
    ocean_out[1, 0] += DRAG_COEF * (push_y - ocean[1, 0] * cover)

    for n in others:

        @pl.when(inside[n])
        def _(n=n):
            msg_copy(n).wait_send()
            flux_copy(n).wait_send()

    for side in range(4):

        @pl.when(inside[sides[side]])
        def _(side=side):
            halo_copy(side).wait_send()


def shards(mesh_shape, *args):
    ocean_state, floe_state, _, contact_pairs, bond_ends = args[:5]
    couple_cell = args[8]
    fields, levels, width_x, width_y = ocean_state.shape
    tiles, pairs = contact_pairs.shape[1:]
    bond_count = bond_ends.shape[2]
    floes = floe_state.shape[1]
    tile = floes // tiles
    buckets, slots = couple_cell.shape[1:]
    assert width_x == 8 and 2 * tiles == 8 and tile == slots == width_y == 128
    vmem = pl.BlockSpec(memory_space=pltpu.VMEM)
    dma = pltpu.SemaphoreType.DMA
    return pl.pallas_call(
        functools.partial(kernel, mesh_shape),
        out_shape=(
            jax.ShapeDtypeStruct(ocean_state.shape, F32),
            jax.ShapeDtypeStruct(floe_state.shape, F32),
        ),
        in_specs=[vmem] * 9,
        out_specs=(vmem, vmem),
        scratch_shapes=[
            pltpu.VMEM((buckets, 8, slots), F32),
            pltpu.VMEM((buckets, 8, slots), F32),
            pltpu.VMEM((buckets, 8, slots), F32),
            pltpu.VMEM((buckets, 8, slots), F32),
            pltpu.VMEM((2, fields * levels, width_y), F32),
            pltpu.VMEM((2, fields * levels, width_y), F32),
            pltpu.VMEM((2, fields, width_x, width_y), F32),
            pltpu.VMEM((2, fields, width_x, width_y), F32),
            pltpu.VMEM((floes, pairs + bond_count), BF16),
            pltpu.VMEM((tile, buckets * slots), BF16),
            pltpu.VMEM((width_y, buckets * slots), BF16),
            pltpu.VMEM((2, 2 * tiles, tile), F32),
            pltpu.VMEM((2, 2 * tiles, tile), F32),
            pltpu.VMEM((2, width_x, width_y), F32),
            dma((buckets,)),
            dma((buckets,)),
            dma((buckets,)),
            dma((buckets,)),
            dma((4,)),
            dma((4,)),
        ],
        compiler_params=pltpu.CompilerParams(
            collective_id=0, has_side_effects=True, vmem_limit_bytes=24 * 1024 * 1024
        ),
        cost_estimate=pl.CostEstimate(
            flops=200_000_000, bytes_accessed=1_000_000, transcendentals=0
        ),
    )(*args)


def solution(mesh):
    in_specs = (
        P(None, None, "ocx", "ocy"),
        P(None, ("ocx", "ocy")),
        P(None, ("ocx", "ocy")),
        P(None, ("ocx", "ocy"), None),
        P(None, ("ocx", "ocy"), None),
        P(("ocx", "ocy"), None),
        P(("ocx", "ocy"), None, None),
        P(("ocx", "ocy"), None, None),
        P(("ocx", "ocy"), None, None),
    )
    out_specs = (P(None, None, "ocx", "ocy"), P(None, ("ocx", "ocy")))
    body = functools.partial(shards, (mesh.shape["ocx"], mesh.shape["ocy"]))
    return jax.shard_map(body, mesh=mesh, in_specs=in_specs, out_specs=out_specs, check_vma=False)
```

time: 122 us -> 18.1 us (0.15)
  starting transfers between devices: 34.4 us -> 0 us
  matrix products: 31.9 us -> 0 us
  other arithmetic: 20.6 us -> 0 us
  waiting for transfers between devices: 18.5 us -> 0 us
  Pallas kernels: 0 us -> 12 us
  local copies, waits for them, and re-layouts: 14.6 us -> 5.06 us
    ppermute x12 -> x0, starting transfers between devices: 34.4 us -> none  [the longest x6 24.7 us: with_halo(): before = lax.ppermute(last, axis, up)]
    dot_general x40 -> x0, matrix products: 31.9 us -> none  [the longest x14 17.4 us: pick_rows(): jnp.einsum('tpf,ctf->ctp', table, field, precision=EXACT, preferred_eleme...]
    ppermute x12 -> x0, waiting for transfers between devices: 18.5 us -> none  [the longest x6 18.5 us: with_halo(): before = lax.ppermute(last, axis, up)]
    scatter-add x4 -> x0, other arithmetic: 17.6 us -> none  [the longest x1 9.18 us: floe_side(): jnp.zeros((floe_count,), jnp.float32).at[floe_index].add(weight)]
    pallas_call x0 -> x1, Pallas kernels: none -> 12 us  [shards(): pl.pallas_call(functools.partial(kernel, mesh_shape), out_shape=(jax.Shap...]
    gather x4 -> x0, local copies, waits for them, and re-layouts: 9.95 us -> none  [the longest x2 7.3 us: floe_side(): salt_flux = SALT_COEF * weight * floe_props[1][floe_index]]
    unnamed x23 -> x17, local copies, waits for them, and re-layouts: 2.78 us -> 5.06 us
    slice x9 -> x0, local copies, waits for them, and re-layouts: 1.59 us -> none  [the longest x2 1.08 us: with_halo(): last = lax.slice_in_dim(array, length - width, length, axis=dim)]
  transfers between devices with their start and end apart: 12 -> 0, of which waited for: 2 -> 0; matrix products, arithmetic and copies ran while one was open for 51% -> 0% of each run, Pallas kernels for 0% -> 0%
where the time goes in v1:
time: 18.1 us; the launch traced here: 17.8 us
  Pallas kernels  12 us (66%)
  local copies, waits for them, and re-layouts  5.06 us (28%)
  between operations  0.67 us (4%)
    pallas_call x1, Pallas kernels, shards(): pl.pallas_call(functools.partial(kernel, mesh_shape), out_shape=(jax.Shap...  12 us
    unnamed x17, local copies, waits for them, and re-layouts  5.06 us

profile of v1, /device:TPU:1, one launch (start us, length us, event | category | flops | bytes accessed | tf_op | source)
XLA Modules:
  0.0 17.8 jit_solution(6747038398841222790)
XLA Ops:
  0.6 0.0 copy-start.1
  0.6 0.7 %copy.11.c_floe = s32[1,9,128]{2,1,0:T(8,128)S(1)} copy(s32[1,9,128]{2,0,1:T(1,128)} %param.15) | data formatting | bytes 9216 | tf_op args[6]
  1.3 0.0 copy-start.3
  1.3 0.7 %copy.12.c_weight = f32[1,9,128]{2,1,0:T(8,128)S(1)} copy(f32[1,9,128]{2,0,1:T(1,128)} %param.16) | data formatting | bytes 9216 | tf_op args[7]
  2.0 0.0 copy-start.2
  2.0 0.0 copy-start.4
  2.0 0.7 %copy.13.c_cell = s32[1,9,128]{2,1,0:T(8,128)S(1)} copy(s32[1,9,128]{2,0,1:T(1,128)} %param.17) | data formatting | bytes 9216 | tf_op args[8]
  2.8 0.0 copy-done.1
  2.8 0.0 copy-done.3
  2.8 0.0 copy-done.2
  2.8 0.0 copy-done.4
  2.8 0.0 copy-start
  2.8 0.9 %copy-done = f32[4,16,8,128]{3,2,1,0:T(8,128)S(1)} copy-done((f32[4,16,8,128]{3,2,1,0:T(8,128)S(1)}, f32[4,16,8,128]{3,2,1,0:T(8,128)}, u32[]{:S(2)}) %copy-start) | copy-done | bytes 262168
  3.7 0.0 copy-start.5
  3.7 0.7 %copy-done.5 = s32[4,256]{1,0:T(4,128)S(1)} copy-done((s32[4,256]{1,0:T(4,128)S(1)}, s32[4,256]{1,0:T(4,128)}, u32[]{:S(2)}) %copy-start.5) | copy-done | bytes 4120
  4.4 12.0 %shard_map.104 = (f32[4,16,8,128]{3,2,1,0:T(8,128)S(1)}, f32[4,512]{1,0:T(4,128)S(1)}) custom-call(f32[4,16,8,128]{3,2,1,0:T(8,128)S(1)} %copy-done, f32[4,512]{1,0:T(4,128)S(1)} %copy-done.2, f32[2,512]{1,0:T(2,128)S(1)} %copy-done.4, s32[2,4,512]{2,1,0:T(4,128)S(1)} %copy-done.1, s32[2,4,256]{2,1,0:T(4,128)S(1)} %copy-done.3, s32[4,256]{1,0:T(4,128)S(1)} %copy-done.5, ...), custom_call_target="tpu_custom_call" | custom-call | flops 200000000 | bytes 1000000 | tf_op jit(solution)/shard_map/pallas_call | solution.py:455
  16.5 0.7 %copy.16 = f32[4,16,8,128]{3,2,1,0:T(8,128)} copy(f32[4,16,8,128]{3,2,1,0:T(8,128)S(1)} %get-tuple-element.4) | data formatting | bytes 524288
  17.2 0.6 %copy.17 = f32[4,512]{1,0:T(4,128)} copy(f32[4,512]{1,0:T(4,128)S(1)} %get-tuple-element.5) | data formatting | bytes 16384
Async XLA Ops:
  0.6 2.1 %copy-start.1 = (s32[2,4,512]{2,1,0:T(4,128)S(1)}, s32[2,4,512]{2,1,0:T(4,128)}, u32[]{:S(2)}) copy-start(s32[2,4,512]{2,1,0:T(4,128)} %contact.1) | copy-start | bytes 49156
  1.3 1.4 %copy-start.3 = (s32[2,4,256]{2,1,0:T(4,128)S(1)}, s32[2,4,256]{2,1,0:T(4,128)}, u32[]{:S(2)}) copy-start(s32[2,4,256]{2,1,0:T(4,128)} %bonds.1) | copy-start | bytes 24580
  2.0 0.7 %copy-start.2 = (f32[4,512]{1,0:T(4,128)S(1)}, f32[4,512]{1,0:T(4,128)}, u32[]{:S(2)}) copy-start(f32[4,512]{1,0:T(4,128)} %floe_state.1) | copy-start | bytes 24580
  2.0 0.7 %copy-start.4 = (f32[2,512]{1,0:T(2,128)S(1)}, f32[2,512]{1,0:T(2,128)}, u32[]{:S(2)}) copy-start(f32[2,512]{1,0:T(2,128)} %floe_props.1) | copy-start | bytes 12292
  2.8 1.0 %copy-start = (f32[4,16,8,128]{3,2,1,0:T(8,128)S(1)}, f32[4,16,8,128]{3,2,1,0:T(8,128)}, u32[]{:S(2)}) copy-start(f32[4,16,8,128]{3,2,1,0:T(8,128)} %ocean.1) | copy-start | bytes 786436
  3.7 0.7 %copy-start.5 = (s32[4,256]{1,0:T(4,128)S(1)}, s32[4,256]{1,0:T(4,128)}, u32[]{:S(2)}) copy-start(s32[4,256]{1,0:T(4,128)} %broken.1) | copy-start | bytes 12292

commit v2 on v1

--- a/solution.py
+++ b/solution.py
@@ -61,15 +61,15 @@
 
 def kernel(
     mesh_shape,
-    ocean,
-    floe_state,
-    floe_props,
-    contact,
-    bonds,
-    broken,
-    c_floe,
-    c_weight,
-    c_cell,
+    ocean_hbm,
+    floe_state_hbm,
+    floe_props_hbm,
+    contact_hbm,
+    bonds_hbm,
+    broken_hbm,
+    c_floe_hbm,
+    c_weight_hbm,
+    c_cell_hbm,
     ocean_out,
     floe_out,
     msg,
@@ -85,7 +85,17 @@
     cell_table,
     state,
     props,
-    tend,
+    ocean,
+    surface,
+    floe_state,
+    floe_props,
+    contact,
+    bonds,
+    broken,
+    c_floe,
+    c_weight,
+    c_cell,
+    load_sem,
     msg_send,
     msg_recv,
     flux_send,
@@ -96,7 +106,7 @@
     size_x, size_y = mesh_shape
     fields, levels, width_x, width_y = ocean.shape
     planes = fields * levels
-    buckets, slots = c_cell.shape[1], c_cell.shape[2]
+    buckets, slots = c_cell.shape[0], c_cell.shape[2]
     tiles, pairs = contact.shape[1], contact.shape[2]
     bond_count = bonds.shape[2]
     tile = floe_state.shape[1] // tiles
@@ -121,6 +131,26 @@
         @pl.when(inside[n])
         def _(n=n):
             pl.semaphore_signal(barrier, inc=1, device_id=place(n), device_id_type=MESH)
+
+    loads = [
+        pltpu.make_async_copy(src, dst, load_sem.at[at])
+        for at, (src, dst) in enumerate(
+            [
+                (c_cell_hbm, c_cell),
+                (ocean_hbm.at[pl.ds(0, 2), 0], surface),
+                (c_floe_hbm, c_floe),
+                (floe_props_hbm, floe_props),
+                (c_weight_hbm, c_weight),
+                (floe_state_hbm, floe_state),
+                (ocean_hbm, ocean),
+                (contact_hbm, contact),
+                (bonds_hbm, bonds),
+                (broken_hbm, broken),
+            ]
+        )
+    ]
+    for load in loads:
+        load.start()
 
     def copy(src, dst, send, recv, n):
         return pltpu.make_async_remote_copy(
@@ -175,6 +205,9 @@
     def wide(ref_row):
         return jnp.broadcast_to(ref_row, (8, slots))
 
+    for load in loads[:6]:
+        load.wait()
+
     for t in range(tiles):
         lanes = pl.ds(t * tile, tile)
         for c in range(2):
@@ -182,16 +215,16 @@
             state[1, pl.ds(c * tiles + t, 1), :] = floe_state[pl.ds(2 + c, 1), lanes]
             props[0, pl.ds(c * tiles + t, 1), :] = floe_props[pl.ds(0, 1), lanes]
             props[1, pl.ds(c * tiles + t, 1), :] = floe_props[pl.ds(1, 1), lanes]
-    east, north = ocean[0, 0], ocean[1, 0]
+    east, north = surface[0], surface[1]
     thick = props[1]
     floe_lane, floe_mask = [], []
     for n in range(buckets):
-        cell = wide(c_cell[0, pl.ds(n, 1), :])
+        cell = wide(c_cell[n])
         cell_row, cell_lane = cell // width_y, cell % width_y
-        floe = wide(c_floe[0, pl.ds(n, 1), :])
+        floe = wide(c_floe[n])
         floe_lane.append(floe % tile)
         floe_mask.append(floe // tile == row_tile)
-        weight = wide(c_weight[0, pl.ds(n, 1), :])
+        weight = wide(c_weight[n])
         here = cell_row == row8
         first = jnp.where(here, lane_gather(east, cell_lane), 0.0)
         second = jnp.where(here, lane_gather(north, cell_lane), 0.0)
@@ -215,6 +248,8 @@
             msg_copy(n).start()
 
     msg_in[CENTRE] = msg[CENTRE]
+    for load in loads[6:]:
+        load.wait()
 
     flat = ocean.reshape(planes * width_x, width_y)
     row_out[0] = flat[pl.ds(0, planes, stride=width_x), :]
@@ -236,8 +271,8 @@
 
     low_row = lax.broadcasted_iota(jnp.int32, (tile, slots), 0)
     for n in range(buckets):
-        floe = c_floe[0, pl.ds(n, 1), :] % tile
-        cell = c_cell[0, pl.ds(n, 1), :] % width_y
+        floe = c_floe[n] % tile
+        cell = c_cell[n] % width_y
         lanes = pl.ds(n * slots, slots)
         floe_table[:, lanes] = hot(low_row == floe).astype(BF16)
         cell_table[:, lanes] = hot(low_row == cell).astype(BF16)
@@ -297,7 +332,7 @@
         total = product(split(jnp.concatenate(values, axis=1)), floe_table[...])
         return total[:rows] + total[rows:]
 
-    weights = [wide(c_weight[0, pl.ds(n, 1), :]) for n in range(buckets)]
+    weights = [wide(c_weight[n]) for n in range(buckets)]
     masked = [jnp.where(m, w, 0.0) for m, w in zip(floe_mask, weights)]
     area = DRAG_COEF * per_floe(masked)
 
@@ -346,7 +381,7 @@
             floe_out[pl.ds(2 + c, 1), lanes] = state[1, pl.ds(c * tiles + t, 1), :]
 
     here = [
-        c_cell[0, pl.ds(n, 1), :] // width_y == row8 for n in range(buckets)
+        c_cell[n] // width_y == row8 for n in range(buckets)
     ]
 
     def per_cell(ref, first, second):
@@ -441,6 +476,7 @@
 
 
 def shards(mesh_shape, *args):
+    args = args[:6] + tuple(a.transpose(1, 0, 2) for a in args[6:])
     ocean_state, floe_state, _, contact_pairs, bond_ends = args[:5]
     couple_cell = args[8]
     fields, levels, width_x, width_y = ocean_state.shape
@@ -448,7 +484,7 @@
     bond_count = bond_ends.shape[2]
     floes = floe_state.shape[1]
     tile = floes // tiles
-    buckets, slots = couple_cell.shape[1:]
+    buckets, _, slots = couple_cell.shape
     assert width_x == 8 and 2 * tiles == 8 and tile == slots == width_y == 128
     vmem = pl.BlockSpec(memory_space=pltpu.VMEM)
     dma = pltpu.SemaphoreType.DMA
@@ -458,7 +494,7 @@
             jax.ShapeDtypeStruct(ocean_state.shape, F32),
             jax.ShapeDtypeStruct(floe_state.shape, F32),
         ),
-        in_specs=[vmem] * 9,
+        in_specs=[pl.BlockSpec(memory_space=pltpu.HBM)] * 9,
         out_specs=(vmem, vmem),
         scratch_shapes=[
             pltpu.VMEM((buckets, 8, slots), F32),
@@ -474,7 +510,10 @@
             pltpu.VMEM((width_y, buckets * slots), BF16),
             pltpu.VMEM((2, 2 * tiles, tile), F32),
             pltpu.VMEM((2, 2 * tiles, tile), F32),
+            pltpu.VMEM(ocean_state.shape, F32),
             pltpu.VMEM((2, width_x, width_y), F32),
+            *[pltpu.VMEM(a.shape, a.dtype) for a in args[1:]],
+            dma((10,)),
             dma((buckets,)),
             dma((buckets,)),
             dma((buckets,)),
@@ -483,7 +522,7 @@
             dma((4,)),
         ],
         compiler_params=pltpu.CompilerParams(
-            collective_id=0, has_side_effects=True, vmem_limit_bytes=24 * 1024 * 1024
+            collective_id=0, has_side_effects=True, vmem_limit_bytes=56 * 1024 * 1024
         ),
         cost_estimate=pl.CostEstimate(
             flops=200_000_000, bytes_accessed=1_000_000, transcendentals=0

time: 18.1 us -> 16 us (0.88)
  local copies, waits for them, and re-layouts: 5.06 us -> 2.28 us
  Pallas kernels: 12 us -> 12.9 us
    unnamed x17 -> x4, local copies, waits for them, and re-layouts: 5.06 us -> 2.28 us
    pallas_call x1, Pallas kernels: 12 us -> 12.9 us  [shards(): pl.pallas_call(functools.partial(kernel, mesh_shape), out_shape=(jax.Shap...]
where the time goes in v2:
time: 16 us; the launch traced here: 15.8 us
  Pallas kernels  12.9 us (81%)
  local copies, waits for them, and re-layouts  2.28 us (14%)
  between operations  0.65 us (4%)
    pallas_call x1, Pallas kernels, shards(): pl.pallas_call(functools.partial(kernel, mesh_shape), out_shape=(jax.Shap...  12.9 us
    unnamed x4, local copies, waits for them, and re-layouts  2.28 us

profile of v2, /device:TPU:1, one launch (start us, length us, event | category | flops | bytes accessed | tf_op | source)
XLA Modules:
  0.0 15.8 jit_solution(15008289000467766556)
XLA Ops:
  0.6 12.9 %shard_map.104 = (f32[4,16,8,128]{3,2,1,0:T(8,128)}, f32[4,512]{1,0:T(4,128)}) custom-call(f32[4,16,8,128]{3,2,1,0:T(8,128)} %ocean_hbm.1, f32[4,512]{1,0:T(4,128)} %floe_state_hbm.1, f32[2,512]{1,0:T(2,128)} %floe_props_hbm.1, s32[2,4,512]{2,1,0:T(4,128)} %contact_hbm.1, s32[2,4,256]{2,1,0:T(4,128)} %bonds_hbm.1, s32[4,256]{1,0:T(4,128)} %broken_hbm.1, ...), custom_call_target="tpu_custom_call" | custom-call | flops 200000000 | bytes 1000000 | tf_op jit(solution)/shard_map/pallas_call | solution.py:491
  13.5 0.0 copy-start
  13.5 1.7 %copy.13 = f32[4,16,8,128]{3,2,1,0:T(8,128)} copy(f32[4,16,8,128]{3,2,1,0:T(8,128)} %get-tuple-element.4) | data formatting | bytes 524288
  15.2 0.0 copy-done
  15.2 0.6 %copy.14 = f32[4,512]{1,0:T(4,128)} copy(f32[4,512]{1,0:T(4,128)S(1)} %copy-done) | data formatting | bytes 16384
Async XLA Ops:
  13.5 1.7 %copy-start = (f32[4,512]{1,0:T(4,128)S(1)}, f32[4,512]{1,0:T(4,128)}, u32[]{:S(2)}) copy-start(f32[4,512]{1,0:T(4,128)} %get-tuple-element.5) | copy-start | bytes 24580

commit v3 on v2

--- a/solution.py
+++ b/solution.py
@@ -119,7 +119,7 @@
         ok_x = {-1: at_x > 0, 0: at_x >= 0, 1: at_x < size_x - 1}[dx]
         ok_y = {-1: at_y > 0, 0: at_y >= 0, 1: at_y < size_y - 1}[dy]
         inside.append(jnp.logical_and(ok_x, ok_y))
-    others = [n for n in range(buckets) if n != CENTRE]
+    others = [0, 2, 6, 8, 1, 7, 3, 5]
     sides = [1, 7, 3, 5]
 
     def place(n):
@@ -248,6 +248,20 @@
             msg_copy(n).start()
 
     msg_in[CENTRE] = msg[CENTRE]
+    for n in others:
+
+        @pl.when(jnp.logical_not(inside[n]))
+        def _(n=n):
+            msg_in[n] = jnp.zeros((8, slots), F32)
+            flux_in[n] = jnp.zeros((8, slots), F32)
+
+    for side in range(4):
+
+        @pl.when(jnp.logical_not(inside[sides[side]]))
+        def _(side=side):
+            dst = row_in if side < 2 else col_in
+            dst[side % 2] = jnp.zeros(dst.shape[1:], F32)
+
     for load in loads[6:]:
         load.wait()
 
@@ -285,9 +299,9 @@
             lanes = pl.ds(at * span, span)
             head = ref[0, pl.ds(t, 1), lanes]
             tail = ref[1, pl.ds(t, 1), lanes]
-            pair_table[pl.ds(t * tile, tile), pl.ds(c * span, span)] = (
-                hot(wide_row == head) - hot(wide_row == tail)
-            ).astype(BF16)
+            pair_table[pl.ds(c * span, span), pl.ds(t * tile, tile)] = (
+                (hot(wide_row == head) - hot(wide_row == tail)).T.astype(BF16)
+            )
 
     def twice(array):
         return jnp.concatenate([array, array], axis=0)
@@ -319,7 +333,7 @@
             forces.append(depth * (CONTACT_DAMP * relative - CONTACT_STIFF * separation))
         for (head, tail), coef in zip(bond_ends, bond_coef):
             forces.append(coef * (lane_gather(velocity, tail) - lane_gather(velocity, head)))
-        spread = product(split(jnp.concatenate(forces, axis=1)), pair_table[...])
+        spread = jnp.dot(split(jnp.concatenate(forces, axis=1)), pair_table[...], preferred_element_type=F32)
         spread = spread[:rows] + spread[rows:]
         total = jnp.zeros((rows, tile), F32)
         for t in range(tiles):
@@ -341,10 +355,6 @@
         @pl.when(inside[n])
         def _(n=n):
             msg_arrival(n).wait_recv()
-
-        @pl.when(jnp.logical_not(inside[n]))
-        def _(n=n):
-            msg_in[n] = jnp.zeros((8, slots), F32)
 
     samples = [
         jnp.where(low, wide(msg_in[n, pl.ds(0, 1), :]), wide(msg_in[n, pl.ds(4, 1), :]))
@@ -406,11 +416,6 @@
         @pl.when(inside[sides[side]])
         def _(side=side):
             halo_arrival(side).wait_recv()
-
-        @pl.when(jnp.logical_not(inside[sides[side]]))
-        def _(side=side):
-            dst = row_in if side < 2 else col_in
-            dst[side % 2] = jnp.zeros(dst.shape[1:], F32)
 
     rows_f = lax.broadcasted_iota(jnp.int32, (fields, 8, width_y), 1)
     top, bottom = rows_f == 0, rows_f == width_x - 1
@@ -453,10 +458,6 @@
         def _(n=n):
             flux_arrival(n).wait_recv()
 
-        @pl.when(jnp.logical_not(inside[n]))
-        def _(n=n):
-            flux_in[n] = jnp.zeros((8, slots), F32)
-
     push_x, push_y = per_cell(flux_in, 0, 4)
     ocean_out[0, 0] += DRAG_COEF * (push_x - ocean[0, 0] * cover)
     ocean_out[1, 0] += DRAG_COEF * (push_y - ocean[1, 0] * cover)
@@ -473,6 +474,15 @@
         @pl.when(inside[sides[side]])
         def _(side=side):
             halo_copy(side).wait_send()
+
+
+def store(ocean, floes, ocean_out, floe_out, sem):
+    first = pltpu.make_async_copy(ocean, ocean_out, sem.at[0])
+    second = pltpu.make_async_copy(floes, floe_out, sem.at[1])
+    first.start()
+    second.start()
+    first.wait()
+    second.wait()
 
 
 def shards(mesh_shape, *args):
@@ -488,11 +498,11 @@
     assert width_x == 8 and 2 * tiles == 8 and tile == slots == width_y == 128
     vmem = pl.BlockSpec(memory_space=pltpu.VMEM)
     dma = pltpu.SemaphoreType.DMA
-    return pl.pallas_call(
+    results = pl.pallas_call(
         functools.partial(kernel, mesh_shape),
         out_shape=(
-            jax.ShapeDtypeStruct(ocean_state.shape, F32),
-            jax.ShapeDtypeStruct(floe_state.shape, F32),
+            pltpu.VMEM(ocean_state.shape, F32),
+            pltpu.VMEM(floe_state.shape, F32),
         ),
         in_specs=[pl.BlockSpec(memory_space=pltpu.HBM)] * 9,
         out_specs=(vmem, vmem),
@@ -505,7 +515,7 @@
             pltpu.VMEM((2, fields * levels, width_y), F32),
             pltpu.VMEM((2, fields, width_x, width_y), F32),
             pltpu.VMEM((2, fields, width_x, width_y), F32),
-            pltpu.VMEM((floes, pairs + bond_count), BF16),
+            pltpu.VMEM((pairs + bond_count, floes), BF16),
             pltpu.VMEM((tile, buckets * slots), BF16),
             pltpu.VMEM((width_y, buckets * slots), BF16),
             pltpu.VMEM((2, 2 * tiles, tile), F32),
@@ -528,6 +538,18 @@
             flops=200_000_000, bytes_accessed=1_000_000, transcendentals=0
         ),
     )(*args)
+    results = [pltpu.with_memory_space_constraint(r, pltpu.VMEM) for r in results]
+    hbm = pl.BlockSpec(memory_space=pltpu.HBM)
+    return pl.pallas_call(
+        store,
+        out_shape=(
+            jax.ShapeDtypeStruct(ocean_state.shape, F32),
+            jax.ShapeDtypeStruct(floe_state.shape, F32),
+        ),
+        in_specs=[vmem] * 2,
+        out_specs=(hbm, hbm),
+        scratch_shapes=[dma((2,))],
+    )(*results)
 
 
 def solution(mesh):

time: 16 us -> 13.5 us (0.84)
  local copies, waits for them, and re-layouts: 2.28 us -> 0 us
  Pallas kernels: 12.9 us -> 12.7 us
    unnamed x4 -> x0, local copies, waits for them, and re-layouts: 2.28 us -> none
    pallas_call x1 -> x2, Pallas kernels: 12.9 us -> 12.7 us  [the longest x1 12 us: shards(): pl.pallas_call(functools.partial(kernel, mesh_shape), out_shape=(pltpu.VM...]
where the time goes in v3:
time: 13.5 us; the launch traced here: 13.3 us
  Pallas kernels  12.7 us (94%)
  between operations  0.64 us (5%)
    pallas_call x1, Pallas kernels, shards(): pl.pallas_call(functools.partial(kernel, mesh_shape), out_shape=(pltpu.VM...  12 us
    pallas_call x1, Pallas kernels, shards(): pl.pallas_call(store, out_shape=(jax.ShapeDtypeStruct(ocean_state.shape,...  0.72 us

profile of v3, /device:TPU:1, one launch (start us, length us, event | category | flops | bytes accessed | tf_op | source)
XLA Modules:
  0.0 13.3 jit_solution(781406306780604257)
XLA Ops:
  0.6 12.0 %shard_map.104 = (f32[4,16,8,128]{3,2,1,0:T(8,128)S(1)}, f32[4,512]{1,0:T(4,128)S(1)}) custom-call(f32[4,16,8,128]{3,2,1,0:T(8,128)} %ocean_hbm.1, f32[4,512]{1,0:T(4,128)} %floe_state_hbm.1, f32[2,512]{1,0:T(2,128)} %floe_props_hbm.1, s32[2,4,512]{2,1,0:T(4,128)} %contact_hbm.1, s32[2,4,256]{2,1,0:T(4,128)} %bonds_hbm.1, s32[4,256]{1,0:T(4,128)} %broken_hbm.1, ...), custom_call_target="tpu_custom_call" | custom-call | flops 200000000 | bytes 1000000 | tf_op jit(solution)/shard_map/pallas_call | solution.py:501
  12.6 0.7 %shard_map.105 = (f32[4,16,8,128]{3,2,1,0:T(8,128)}, f32[4,512]{1,0:T(4,128)}) custom-call(f32[4,16,8,128]{3,2,1,0:T(8,128)S(1)} %get-tuple-element.4.ocean, f32[4,512]{1,0:T(4,128)S(1)} %get-tuple-element.5.floes), custom_call_target="tpu_custom_call" | custom-call | tf_op jit(solution)/shard_map/pallas_call | solution.py:543

commit v4 on v3

--- a/solution.py
+++ b/solution.py
@@ -51,7 +51,7 @@
 
 def product(values, table):
     return lax.dot_general(
-        values, table, (((1,), (1,)), ((), ())), preferred_element_type=F32
+        values, table, (((1,), (0,)), ((), ())), preferred_element_type=F32
     )
 
 
@@ -286,10 +286,8 @@
     low_row = lax.broadcasted_iota(jnp.int32, (tile, slots), 0)
     for n in range(buckets):
         floe = c_floe[n] % tile
-        cell = c_cell[n] % width_y
         lanes = pl.ds(n * slots, slots)
-        floe_table[:, lanes] = hot(low_row == floe).astype(BF16)
-        cell_table[:, lanes] = hot(low_row == cell).astype(BF16)
+        floe_table[lanes, :] = hot(low_row == floe).T.astype(BF16)
     span = 128
     contact_chunks, bond_chunks = pairs // span, bond_count // span
     wide_row = lax.broadcasted_iota(jnp.int32, (tile, span), 0)
@@ -409,6 +407,9 @@
         total = total[:16] + total[16:]
         return total[:8], total[8:]
 
+    for n in range(buckets):
+        cells = hot(low_row == c_cell[n] % width_y)
+        cell_table[pl.ds(n * slots, slots), :] = cells.T.astype(BF16)
     cover, salt = per_cell(msg_in, 1, 2)
 
     for side in range(4):
@@ -516,8 +517,8 @@
             pltpu.VMEM((2, fields, width_x, width_y), F32),
             pltpu.VMEM((2, fields, width_x, width_y), F32),
             pltpu.VMEM((pairs + bond_count, floes), BF16),
-            pltpu.VMEM((tile, buckets * slots), BF16),
-            pltpu.VMEM((width_y, buckets * slots), BF16),
+            pltpu.VMEM((buckets * slots, tile), BF16),
+            pltpu.VMEM((buckets * slots, width_y), BF16),
             pltpu.VMEM((2, 2 * tiles, tile), F32),
             pltpu.VMEM((2, 2 * tiles, tile), F32),
             pltpu.VMEM(ocean_state.shape, F32),

time: 13.5 us -> 13.3 us (0.985)
  Pallas kernels: 12.7 us -> 12.5 us
    pallas_call x1, Pallas kernels: 12 us -> 11.8 us  [shards(): pl.pallas_call(functools.partial(kernel, mesh_shape), out_shape=(pltpu.VM...]
where the time goes in v4:
time: 13.3 us; the launch traced here: 13.1 us
  Pallas kernels  12.5 us (94%)
  between operations  0.64 us (5%)
    pallas_call x1, Pallas kernels, shards(): pl.pallas_call(functools.partial(kernel, mesh_shape), out_shape=(pltpu.VM...  11.8 us
    pallas_call x1, Pallas kernels, shards(): pl.pallas_call(store, out_shape=(jax.ShapeDtypeStruct(ocean_state.shape,...  0.72 us

profile of v4, /device:TPU:1, one launch (start us, length us, event | category | flops | bytes accessed | tf_op | source)
XLA Modules:
  0.0 13.1 jit_solution(16341553187622681728)
XLA Ops:
  0.6 11.8 %shard_map.104 = (f32[4,16,8,128]{3,2,1,0:T(8,128)S(1)}, f32[4,512]{1,0:T(4,128)S(1)}) custom-call(f32[4,16,8,128]{3,2,1,0:T(8,128)} %ocean_hbm.1, f32[4,512]{1,0:T(4,128)} %floe_state_hbm.1, f32[2,512]{1,0:T(2,128)} %floe_props_hbm.1, s32[2,4,512]{2,1,0:T(4,128)} %contact_hbm.1, s32[2,4,256]{2,1,0:T(4,128)} %bonds_hbm.1, s32[4,256]{1,0:T(4,128)} %broken_hbm.1, ...), custom_call_target="tpu_custom_call" | custom-call | flops 200000000 | bytes 1000000 | tf_op jit(solution)/shard_map/pallas_call | solution.py:502
  12.4 0.7 %shard_map.105 = (f32[4,16,8,128]{3,2,1,0:T(8,128)}, f32[4,512]{1,0:T(4,128)}) custom-call(f32[4,16,8,128]{3,2,1,0:T(8,128)S(1)} %get-tuple-element.4.ocean, f32[4,512]{1,0:T(4,128)S(1)} %get-tuple-element.5.floes), custom_call_target="tpu_custom_call" | custom-call | tf_op jit(solution)/shard_map/pallas_call | solution.py:544
